TPU v7x, 32 devices: a whole 2x2x4 slice. The times are simulated.
32 devices in a mesh: tm: 8 (over y, x, core), depth: 4 (over z).
Axes of the slice: x: 2, y: 2, z: 4, core: 2. Of those that a mesh axis runs over, the one named last changes fastest.
Arguments:
- basis: bfloat16 [32, 16, 8, 2048], P(None, 'depth', None, 'tm'), may hold values from -0.125 to 0.125
- factors: bfloat16 [512, 32], P('tm'), may hold values from -6 to 6
- measured: bfloat16 [512, 8, 2048], P('tm'), may hold values from 0.29882812 to 3
- shear: int32 [512], P('tm'), may hold values from -3 to 3
- window: int32 [512], P('tm'), may hold values from 0 to 1024
Outputs:
- grad_basis: float32 [32, 16, 8, 2048], P(None, 'depth', None, 'tm')
All inputs are finite; a program needn't handle non-finite values.
Results may differ from a plain program's by a relative error of at most 0.0022.
Values may be sent and summed in bfloat16 or wider, within the bound.
A program may use at most 128 MiB of HBM per device.

v0:
```python
import math

import jax
import jax.numpy as jnp
from jax import lax
from jax.sharding import PartitionSpec as P

SHEAR = 3
WD = 1024


def with_halo(cells, sides, width):
    for axis, dim in sides:
        count = lax.axis_size(axis)
        ends = count - 1
        head = lax.slice_in_dim(cells, 0, width, axis=dim)
        tail = lax.slice_in_dim(cells, cells.shape[dim] - width, cells.shape[dim], axis=dim)
        cells = jnp.concatenate(
            [
                lax.ppermute(tail, axis, [(i, (i + 1) % count) for i in range(ends)]),
                cells,
                lax.ppermute(head, axis, [((i + 1) % count, i) for i in range(ends)]),
            ],
            axis=dim,
        )
    return cells


def residual_grad(projection, measure_part, window_part, columns, norm_scale):
    transmit = jnp.exp(-projection)
    inside = (columns[None, None, :] >= window_part[:, None, None]) & (
        columns[None, None, :] < window_part[:, None, None] + WD
    )
    residual = jnp.where(inside, transmit - measure_part.astype(jnp.float32), jnp.float32(0.0))
    return (-transmit * residual * norm_scale).astype(jnp.bfloat16)


def per_device(basis, factors, measured, shear, window):
    rank_count = basis.shape[0]
    local_depth = basis.shape[1]
    slab_rows = basis.shape[2]
    column_shard = basis.shape[3]
    total_depth = local_depth * lax.axis_size("depth")
    margin = SHEAR * (total_depth // 2)
    shear_count = 2 * SHEAR + 1
    depth_ids = (
        lax.axis_index("depth") * local_depth
        + jnp.arange(local_depth, dtype=jnp.int32)
        - total_depth // 2
    )
    frames_total = factors.shape[0] * lax.axis_size("tm")
    norm_scale = 1.0 / math.sqrt(frames_total)
    widened = with_halo(basis, (("tm", 3),), margin)
    frame_factors = lax.all_gather(factors, "tm", axis=0, tiled=True)
    frame_shear, frame_window = (
        lax.all_gather(shear, "tm", axis=0, tiled=True),
        lax.all_gather(window, "tm", axis=0, tiled=True),
    )
    frame_measured = lax.all_to_all(measured, "tm", split_axis=2, concat_axis=0, tiled=True)
    first_column = lax.axis_index("tm") * column_shard
    wide_width = widened.shape[3]
    width_out = wide_width - 2 * margin
    frames_here = frame_factors.shape[0]
    shear_values = jnp.arange(shear_count, dtype=jnp.int32) - SHEAR
    selector = frame_shear[:, None] == shear_values[None, :]
    coef_bf = jnp.where(
        selector[:, :, None], frame_factors[:, None, :], jnp.zeros((), jnp.bfloat16)
    )
    coef_bf = coef_bf.reshape(frames_here, shear_count * rank_count)
    sheared_list = []
    for step in range(shear_count):
        shift_value = step - SHEAR
        running = jnp.zeros((rank_count, slab_rows, width_out), jnp.float32)
        for level in range(local_depth):
            start = margin + shift_value * depth_ids[level]
            piece = lax.dynamic_slice_in_dim(widened[:, level], start, width_out, 2)
            running = running + piece.astype(jnp.float32)
        sheared_list.append(running)
    sheared = jnp.stack(sheared_list, 0).reshape(shear_count * rank_count, slab_rows * width_out)
    ray_parts = jnp.dot(
        coef_bf.astype(jnp.float32),
        sheared,
        precision=lax.Precision.HIGHEST,
        preferred_element_type=jnp.float32,
    )
    ray_parts = ray_parts.reshape(frames_here, slab_rows, width_out)
    columns = first_column + jnp.arange(width_out, dtype=jnp.int32)
    projection = lax.psum(ray_parts, "depth")
    ray_grad = residual_grad(projection, frame_measured, frame_window, columns, norm_scale)
    grad_wide = with_halo(ray_grad, (("tm", 2),), margin)
    spread = lax.dot_general(
        coef_bf,
        grad_wide.reshape(frames_here, slab_rows * wide_width),
        (((0,), (0,)), ((), ())),
        preferred_element_type=jnp.float32,
    )
    spread = spread.reshape(shear_count, rank_count, slab_rows, wide_width)
    level_list = []
    for level in range(local_depth):
        running = jnp.zeros((rank_count, slab_rows, width_out), jnp.float32)
        for step in range(shear_count):
            shift_value = step - SHEAR
            start = margin - shift_value * depth_ids[level]
            running = running + lax.dynamic_slice_in_dim(spread[step], start, width_out, 2)
        level_list.append(running)
    accumulated = jnp.stack(level_list, 1)
    return accumulated


def solution(mesh):
    in_specs = (P(None, "depth", None, "tm"), P("tm", None), P("tm", None, None), P("tm"), P("tm"))
    out_specs = P(None, "depth", None, "tm")
    return jax.shard_map(
        per_device, mesh=mesh, in_specs=in_specs, out_specs=out_specs, check_vma=False
    )
```

profile of v0, /device:TPU:16, one launch (start us, length us, event | category | flops | bytes accessed | tf_op | source)
XLA Modules:
  0.0 255.8 jit_solution(1336982616253657661)
XLA Ops:
  6.5 1.2 fusion.10
  7.8 1.3 collective-permute-start.1
  9.1 3.0 %collective-permute-start = (bf16[32,4,8,24]{3,2,1,0:T(8,128)(2,1)S(1)}, bf16[32,4,8,24]{3,2,1,0:T(8,128)(2,1)S(1)}, u32[]{:S(2)}, u32[]{:S(2)}) collective-permute-start(bf16[32,4,8,24]{3,2,1,0:T(8,128)(2,1)S(1)} %get-tuple-element.25), channel_id=1, source_target_pairs={{0,4},{4,8},{8,12},{12,16},{16,20},{20,24},{24,28},{1,5},{5,9},{9,... | collective-permute-start | bytes 147464 | tf_op jit(solution)/shard_map/ppermute | solution.py:20
  12.1 9.9 %all-gather = bf16[8,64,32]{1,2,0:T(8,128)(2,1)S(1)} all-gather(bf16[1,64,32]{1,2,0:T(8,128)(2,1)} %bitcast.196), channel_id=1, replica_groups=mesh['tm'=8,'depth'=4] {'tm'}, dimensions={0}, use_global_device_ids=true | all-gather | bytes 36864 | tf_op jit(solution)/shard_map/all_gather | solution.py:54
  22.2 1.2 dynamic-slice.24
  24.1 0.9 dynamic-update-slice
  24.9 0.8 dynamic-update-slice.1
  25.8 7.2 %all-reduce.2 = (s32[512]{0:T(512)S(1)}, s32[512]{0:T(512)S(1)}) all-reduce(s32[512]{0:T(512)S(1)} %dynamic-update-slice, s32[512]{0:T(512)S(1)} %dynamic-update-slice.1), channel_id=1, replica_groups=mesh['tm'=8,'depth'=4] {'tm'}, use_global_device_ids=true, to_apply=%add | all-reduce | flops 1024 | bytes 8192
  33.1 0.7 fusion.11
  53.3 4.3 %fusion.4 = f32[512,8,256]{2,0,1:T(8,128)} fusion(bf16[512,224,1]{0,1,2:T(8,128)(2,1)S(1)} %bitcast.194, f32[28,8,8,256]{3,2,1,0:T(8,128)S(1)} %bitcast.193), kind=kOutput, calls=%fused_computation.6 | convolution fusion | flops 2818572288 | bytes 6258688 | tf_op jit(solution)/shard_map/dot_general | solution.py:80
  57.7 1.6 copy-done
  59.2 5.2 %copy.67 = bf16[64,8,2048]{0,1,2:T(8,128)(2,1)} copy(bf16[64,8,2048]{2,1,0:T(8,128)(2,1)S(1)} %copy-done) | data formatting | bytes 4194304 | tf_op args[2]
  64.4 7.6 %reshape.749 = bf16[8,2,65536]{2,1,0:T(2,128)(2,1)} reshape(bf16[2048,8,64]{2,1,0:T(8,128)(2,1)} %bitcast.190) | data formatting | bytes 4194304
  72.0 3.6 %all-to-all-start = ((bf16[8,2,65536]{2,1,0:T(2,128)(2,1)}), bf16[8,2,65536]{2,1,0:T(2,128)(2,1)S(1)}, u32[]{:S(2)}, u32[]{:S(2)}) async-start(bf16[8,2,65536]{2,1,0:T(2,128)(2,1)} %reshape.749), calls=%async_computation | async-start | bytes 4194304 | tf_op jit(solution)/shard_map/all_to_all | solution.py:59
  75.8 26.3 %all-to-all-done = bf16[8,2,65536]{2,1,0:T(2,128)(2,1)S(1)} async-done(((bf16[8,2,65536]{2,1,0:T(2,128)(2,1)}), bf16[8,2,65536]{2,1,0:T(2,128)(2,1)S(1)}, u32[]{:S(2)}, u32[]{:S(2)}) %all-to-all-start) | async-done | bytes 2097184 | tf_op jit(solution)/shard_map/all_to_all | solution.py:59
  102.2 5.0 %reshape.750 = bf16[2048,8,64]{2,1,0:T(8,128)(2,1)} reshape(bf16[8,2,65536]{2,1,0:T(2,128)(2,1)S(1)} %all-to-all-done) | data formatting | bytes 4194304
  107.2 6.1 %copy.68 = f32[64,8,8,256]{3,0,2,1:T(8,128)} copy(bf16[64,8,8,256]{0,1,3,2:T(8,128)(2,1)} %bitcast.191) | data formatting | bytes 6291456 | tf_op jit(solution)/shard_map/convert_element_type | solution.py:34
  113.2 98.7 %all-reduce.5.cloned.1.call-done = f32[512,8,256]{2,0,1:T(8,128)} async-done(((f32[512,8,256]{2,0,1:T(8,128)}), f32[512,8,256]{2,0,1:T(8,128)}) %all-reduce.5.cloned.1.call-update) | async-done | bytes 4194320 | tf_op jit(solution)/shard_map/psum | solution.py:88
  211.9 4.7 %fusion.3 = bf16[512,8,256]{2,0,1:T(8,128)(2,1)S(1)} fusion(f32[64,8,8,256]{3,0,2,1:T(8,128)} %copy.68, f32[512,8,256]{2,0,1:T(8,128)} %all-reduce.5.cloned.1.call-done, pred[512,256]{1,0:T(8,128)(4,1)S(1)} %compare_and_fusion), kind=kLoop, calls=%fused_computation.4 | loop fusion | flops 7340032 | bytes 10616832 | tf_op jit(solution)/shard_map/convert_element_type | solution.py:35
  216.6 1.5 fusion.8
  218.1 2.2 copy.70
  220.3 1.3 collective-permute-start.3
  221.6 1.0 copy.69
  222.6 3.7 %collective-permute-start.2 = (bf16[512,8,24]{0,2,1:T(8,128)(2,1)}, bf16[512,8,24]{0,2,1:T(8,128)(2,1)}, u32[]{:S(2)}, u32[]{:S(2)}) collective-permute-start(bf16[512,8,24]{0,2,1:T(8,128)(2,1)} %copy.69), channel_id=1, source_target_pairs={{0,4},{4,8},{8,12},{12,16},{16,20},{20,24},{24,28},{1,5},{5,9},{9,... | collective-permute-start | bytes 589832 | tf_op jit(solution)/shard_map/ppermute | solution.py:20
  231.3 1.4 copy.72
  232.7 2.2 copy.71
  235.0 4.8 %pad_maximum_fusion = bf16[512,8,304]{2,0,1:T(8,128)(2,1)} fusion(bf16[512,8,24]{2,0,1:T(8,128)(2,1)S(1)} %copy.72, bf16[512,8,256]{2,0,1:T(8,128)(2,1)S(1)} %fusion.3, bf16[512,8,24]{2,0,1:T(8,128)(2,1)} %copy.71), kind=kLoop, calls=%fused_computation.5 | loop fusion | flops 7471104 | bytes 4980736 | tf_op jit(solution)/shard_map/concatenate | solution.py:18
  239.8 3.1 %copy.73 = bf16[512,8,304]{0,2,1:T(8,128)(2,1)S(1)} copy(bf16[512,8,304]{2,0,1:T(8,128)(2,1)} %pad_maximum_fusion) | data formatting | bytes 4980736 | tf_op jit(solution)/shard_map/concatenate | solution.py:18
  242.9 0.9 fusion.12
  245.6 0.6 add_bitcast_fusion
  246.2 0.6 add_bitcast_fusion.1
  247.9 1.1 pad_maximum_fusion.1
  (39 shorter events, 5.6 us)
Async XLA Ops:
  6.5 44.5 %copy-start.1 = (bf16[32,4,8,256]{3,2,1,0:T(8,128)(2,1)S(1)}, bf16[32,4,8,256]{3,2,1,0:T(8,128)(2,1)}, u32[]{:S(2)}) copy-start(bf16[32,4,8,256]{3,2,1,0:T(8,128)(2,1)} %param.5) | copy-start | bytes 1572868
  6.5 205.4 %all-reduce.5.cloned.1.call-start = ((), (), s32[]{:S(2)}) async-start(), calls=%async_computation.1 | async-start | bytes 8388608 | tf_op jit(solution)/shard_map/psum | solution.py:88
  7.8 43.2 %collective-permute-start.1 = (bf16[32,4,8,24]{3,2,1,0:T(8,128)(2,1)S(1)}, bf16[32,4,8,24]{3,2,1,0:T(8,128)(2,1)S(1)}, u32[]{:S(2)}, u32[]{:S(2)}) collective-permute-start(bf16[32,4,8,24]{3,2,1,0:T(8,128)(2,1)S(1)} %get-tuple-element.26), channel_id=1, source_target_pairs={{4,0},{8,4},{12,8},{16,12},{20,16},{24,20},{28,24},{5,1},{9,5},{13... | collective-permute-start | bytes 147464 | tf_op jit(solution)/shard_map/ppermute | solution.py:22
  9.1 41.9 %collective-permute-start = (bf16[32,4,8,24]{3,2,1,0:T(8,128)(2,1)S(1)}, bf16[32,4,8,24]{3,2,1,0:T(8,128)(2,1)S(1)}, u32[]{:S(2)}, u32[]{:S(2)}) collective-permute-start(bf16[32,4,8,24]{3,2,1,0:T(8,128)(2,1)S(1)} %get-tuple-element.25), channel_id=1, source_target_pairs={{0,4},{4,8},{8,12},{12,16},{16,20},{20,24},{24,28},{1,5},{5,9},{9,... | collective-permute-start | bytes 147464 | tf_op jit(solution)/shard_map/ppermute | solution.py:20
  57.6 1.6 copy-start
  72.0 30.2 %all-to-all-start = ((bf16[8,2,65536]{2,1,0:T(2,128)(2,1)}), bf16[8,2,65536]{2,1,0:T(2,128)(2,1)S(1)}, u32[]{:S(2)}, u32[]{:S(2)}) async-start(bf16[8,2,65536]{2,1,0:T(2,128)(2,1)} %reshape.749), calls=%async_computation | async-start | bytes 4194304 | tf_op jit(solution)/shard_map/all_to_all | solution.py:59
  220.3 11.0 %collective-permute-start.3 = (bf16[512,8,24]{0,2,1:T(8,128)(2,1)}, bf16[512,8,24]{0,2,1:T(8,128)(2,1)}, u32[]{:S(2)}, u32[]{:S(2)}) collective-permute-start(bf16[512,8,24]{0,2,1:T(8,128)(2,1)} %copy.70), channel_id=1, source_target_pairs={{4,0},{8,4},{12,8},{16,12},{20,16},{24,20},{28,24},{5,1},{9,5},{13... | collective-permute-start | bytes 589832 | tf_op jit(solution)/shard_map/ppermute | solution.py:22
  222.6 10.2 %collective-permute-start.2 = (bf16[512,8,24]{0,2,1:T(8,128)(2,1)}, bf16[512,8,24]{0,2,1:T(8,128)(2,1)}, u32[]{:S(2)}, u32[]{:S(2)}) collective-permute-start(bf16[512,8,24]{0,2,1:T(8,128)(2,1)} %copy.69), channel_id=1, source_target_pairs={{0,4},{4,8},{8,12},{12,16},{16,20},{20,24},{24,28},{1,5},{5,9},{9,... | collective-permute-start | bytes 589832 | tf_op jit(solution)/shard_map/ppermute | solution.py:20
Sparse Core Ops, SparseCore 0:
  57.8 154.1 all-reduce.4
where the time goes:
time: 260 us; the launch traced here: 256 us
  waiting for transfers between devices  125 us (48%)
  local copies, waits for them, and re-layouts  43.7 us (17%)
  between operations  36.6 us (14%)
  blocking collectives  17.1 us (7%)
  other arithmetic  15.1 us (6%)
  starting transfers between devices  12.9 us (5%)
  matrix products  5.27 us (2%)
    psum x1, waiting for transfers between devices, per_device(): projection = lax.psum(ray_parts, 'depth')  98.7 us
    all_to_all x1, waiting for transfers between devices, per_device(): lax.all_to_all(measured, 'tm', split_axis=2, concat_axis=0, tiled=True)  26.3 us
    unnamed x13, local copies, waits for them, and re-layouts  22.4 us
    all_gather x1, blocking collectives, per_device(): frame_factors = lax.all_gather(factors, 'tm', axis=0, tiled=True)  9.86 us
    unnamed x1, blocking collectives  7.19 us
    ppermute x2, starting transfers between devices, with_halo(): lax.ppermute(tail, axis, [(i, (i + 1) % count) for i in range(ends)])  6.75 us
    convert_element_type x1, local copies, waits for them, and re-layouts, residual_grad(): measure_part.astype(jnp.float32)  6.06 us
    concatenate x2, other arithmetic, with_halo(): jnp.concatenate([lax.ppermute(tail, axis, [(i, (i + 1) % count) for i in...  5.28 us
  transfers between devices with their start and end apart: 6, of which 2 were waited for; matrix products, arithmetic and copies ran while one was open for 12% of the time, Pallas kernels for 0%

commit v1 on v0

v1 whole, which is shorter than its diff:
```python
import functools
import math

import jax
import jax.numpy as jnp
from jax import lax
from jax.experimental import pallas as pl
from jax.experimental.pallas import tpu as pltpu
from jax.sharding import PartitionSpec as P

SHEAR = 3
WD = 1024
LANES = 128
STEPS = 2 * SHEAR + 1


def kernel(
    dims,
    main_ref,
    halo_ref,
    meas_ref,
    out_ref,
    in_main,
    in_halo,
    in_meas,
    back_main,
    back_spill,
    got_main,
    got_spill,
    coef,
    sheared,
    proj,
    grad,
    spread,
    send_main,
    recv_main,
    send_halo,
    recv_halo,
    send_meas,
    recv_meas,
    send_out,
    recv_out,
    send_spill,
    recv_spill,
):
    T, D, LD, HS, C, R, HL, FB = dims
    N = HS * C
    WIDE = C + LANES
    per = LANES // HL
    half = LD * D // 2
    me = lax.axis_index("tm")
    dep = lax.axis_index("depth")
    left = lax.rem(me + T - 1, T)
    right = lax.rem(me + 1, T)

    def peer(base, k, n):
        return lax.rem(base + k, n)

    def at(tm, depth):
        return {"tm": tm, "depth": depth}

    def remote(src, dst, send, recv, where):
        return pltpu.make_async_remote_copy(
            src_ref=src,
            dst_ref=dst,
            send_sem=send,
            recv_sem=recv,
            device_id=where,
            device_id_type=pl.DeviceIdType.MESH,
        )

    barrier = pltpu.get_barrier_semaphore()
    greeted = 0
    for k in range(1, T):
        pl.semaphore_signal(
            barrier, inc=1, device_id=at(peer(me, k, T), dep), device_id_type=pl.DeviceIdType.MESH
        )
        greeted += 1
    for k in range(1, D):
        for tm in (me, left, right):
            pl.semaphore_signal(
                barrier, inc=1, device_id=at(tm, peer(dep, k, D)), device_id_type=pl.DeviceIdType.MESH
            )
            greeted += 1
    in_main[dep] = main_ref[dep]
    in_meas[me] = meas_ref[me]
    pl.semaphore_wait(barrier, greeted)

    def main_copy(k):
        to = peer(dep, k, D)
        return remote(main_ref.at[to], in_main.at[dep], send_main.at[k], recv_main.at[dep], at(me, to))

    def halo_copy(side, k):
        to = peer(dep, k, D)
        return remote(
            halo_ref.at[side, to],
            in_halo.at[side, dep],
            send_halo.at[side, k],
            recv_halo.at[side, dep],
            at((left, right)[side], to),
        )

    def meas_copy(k):
        to = peer(me, k, T)
        return remote(meas_ref.at[to], in_meas.at[me], send_meas.at[k], recv_meas.at[me], at(to, dep))

    sends = []
    for k in list(range(1, D)) + [0]:
        if k:
            sends.append(main_copy(k))
        for side in (0, 1):
            sends.append(halo_copy(side, k))
    for k in range(1, T):
        sends.append(meas_copy(k))
    for copy in sends:
        copy.start()

    for k in range(1, T):
        source = peer(me, k, T)
        remote(
            meas_ref.at[source], in_meas.at[source], send_meas.at[k], recv_meas.at[source], at(source, dep)
        ).wait_recv()

    lane = lax.broadcasted_iota(jnp.int32, (FB, LANES), 1)
    group = (lane // R).astype(jnp.float32)

    def coef_step(j, carry):
        info = in_meas[j, :, N:].astype(jnp.float32)
        first = jnp.where(lane < R, info, 0.0)
        tiled = first
        for q in range(1, LANES // R):
            tiled = tiled + pltpu.roll(first, q * R, 1)
        step = info[:, R : R + 1] + float(SHEAR)
        rows = pl.ds(pl.multiple_of(j * FB, FB), FB)
        for b in range(2):
            coef[rows, b * LANES : (b + 1) * LANES] = jnp.where(
                step == group + float(b * (LANES // R)), tiled, 0.0
            ).astype(jnp.bfloat16)
        return carry

    lax.fori_loop(0, T, coef_step, 0)

    edge = lax.broadcasted_iota(jnp.int32, (R, LANES), 1)
    has_right = me < T - 1
    has_left = me > 0

    sheared[...] = jnp.zeros_like(sheared)
    for q in range(D):

        @pl.when(q != dep)
        def _():
            remote(main_ref.at[q], in_main.at[q], send_main.at[0], recv_main.at[q], at(me, q)).wait_recv()

        for side in (0, 1):
            remote(
                halo_ref.at[side, q],
                in_halo.at[side, q],
                send_halo.at[side, 0],
                recv_halo.at[side, q],
                at((right, left)[side], q),
            ).wait_recv()

        def shear_step(h, carry):
            columns = pl.ds(pl.multiple_of(h * C, LANES), C)
            wides = []
            for l in range(LD):
                g, p = divmod(l, per)
                body = in_main[q, h, l * R : (l + 1) * R, :].astype(jnp.float32)
                after = in_halo[0, q, h, g * R : (g + 1) * R, :].astype(jnp.float32)
                before = in_halo[1, q, h, g * R : (g + 1) * R, :].astype(jnp.float32)
                after = pltpu.roll(after, (LANES - p * HL) % LANES, 1)
                before = pltpu.roll(before, (2 * LANES - HL - p * HL) % LANES, 1)
                rim = jnp.where(
                    jnp.logical_and(edge < HL, has_right),
                    after,
                    jnp.where(jnp.logical_and(edge >= LANES - HL, has_left), before, 0.0),
                )
                wides.append(jnp.concatenate([body, rim], axis=1))
            for s in range(STEPS):
                total = sheared[s * R : (s + 1) * R, columns]
                for l in range(LD):
                    shift = (s - SHEAR) * (q * LD + l - half)
                    turned = pltpu.roll(wides[l], (-shift) % WIDE, 1) if shift else wides[l]
                    total = total + turned[:, :C]
                sheared[s * R : (s + 1) * R, columns] = total
            return carry

        lax.fori_loop(0, HS, shear_step, 0)

    table = sheared[...]
    high = table.astype(jnp.bfloat16)
    low = (table - high.astype(jnp.float32)).astype(jnp.bfloat16)
    proj[...] = jnp.dot(coef[...], high, preferred_element_type=jnp.float32) + jnp.dot(
        coef[...], low, preferred_element_type=jnp.float32
    )

    norm_scale = 1.0 / math.sqrt(T * FB)
    column = lax.broadcasted_iota(jnp.int32, (FB, N), 1)
    column = (lax.rem(column, C) + me * C).astype(jnp.float32)

    def ray_step(j, carry):
        rows = pl.ds(pl.multiple_of(j * FB, FB), FB)
        info = in_meas[j, :, N:].astype(jnp.float32)
        start = info[:, R + 1 : R + 2] + info[:, R + 2 : R + 3]
        transmit = jnp.exp(-proj[rows, :])
        inside = jnp.logical_and(column >= start, column < start + float(WD))
        residual = jnp.where(inside, transmit - in_meas[j, :, :N].astype(jnp.float32), 0.0)
        grad[rows, :] = (-transmit * residual * norm_scale).astype(jnp.bfloat16)
        return carry

    lax.fori_loop(0, T, ray_step, 0)

    spread[...] = lax.dot_general(
        coef[...], grad[...], (((0,), (0,)), ((), ())), preferred_element_type=jnp.float32
    )

    blank = jnp.zeros((R, LANES), jnp.float32)

    def spill_copy(side, q):
        return remote(
            back_spill.at[side, q],
            got_spill.at[side, dep],
            send_spill.at[side, q],
            recv_spill.at[side, dep],
            at((right, left)[side], q),
        )

    def back_copy(q):
        return remote(back_main.at[q], got_main.at[dep], send_out.at[q], recv_out.at[dep], at(me, q))

    for q in range(D):

        def back_step(h, carry):
            columns = pl.ds(pl.multiple_of(h * C, LANES), C)
            totals = [None] * LD
            for s in range(STEPS):
                piece = jnp.concatenate([spread[s * R : (s + 1) * R, columns], blank], axis=1)
                for l in range(LD):
                    shift = (s - SHEAR) * (q * LD + l - half)
                    turned = pltpu.roll(piece, shift % WIDE, 1) if shift else piece
                    totals[l] = turned if s == 0 else totals[l] + turned
            for g in range(LD // per):
                ahead = blank
                behind = blank
                for p in range(per):
                    rim = totals[g * per + p][:, C:]
                    fore = jnp.where(edge < HL, rim, 0.0)
                    aft = jnp.where(edge >= LANES - HL, rim, 0.0)
                    ahead = ahead + (pltpu.roll(fore, p * HL, 1) if p else fore)
                    turn = (p * HL + HL) % LANES
                    behind = behind + (pltpu.roll(aft, turn, 1) if turn else aft)
                back_spill[0, q, h, g * R : (g + 1) * R, :] = ahead.astype(jnp.bfloat16)
                back_spill[1, q, h, g * R : (g + 1) * R, :] = behind.astype(jnp.bfloat16)
            for l in range(LD):
                back_main[q, h, l * R : (l + 1) * R, :] = totals[l][:, :C].astype(jnp.bfloat16)

            @pl.when(q == dep)
            def _():
                for l in range(LD):
                    out_ref[dep * HS + h, l * R : (l + 1) * R, :] = totals[l][:, :C]

            return carry

        lax.fori_loop(0, HS, back_step, 0)

        @pl.when(q != dep)
        def _():
            back_copy(q).start()

        for side in (0, 1):
            spill_copy(side, q).start()

    for k in range(D):
        source = peer(dep, k, D)
        if k:
            remote(
                back_main.at[source], got_main.at[source], send_out.at[0], recv_out.at[source], at(me, source)
            ).wait_recv()
        for side in (0, 1):
            remote(
                back_spill.at[side, source],
                got_spill.at[side, source],
                send_spill.at[side, 0],
                recv_spill.at[side, source],
                at((left, right)[side], source),
            ).wait_recv()

        def gather_step(h, carry):
            for l in range(LD):
                g, p = divmod(l, per)
                rows = slice(l * R, (l + 1) * R)
                if k:
                    total = got_main[source, h, rows, :].astype(jnp.float32)
                else:
                    total = out_ref[source * HS + h, rows, :]
                fore = got_spill[0, source, h, g * R : (g + 1) * R, :].astype(jnp.float32)
                aft = got_spill[1, source, h, g * R : (g + 1) * R, :].astype(jnp.float32)
                fore = pltpu.roll(fore, (LANES - p * HL) % LANES, 1)
                aft = pltpu.roll(aft, (2 * LANES - HL - p * HL) % LANES, 1)
                fore = jnp.where(jnp.logical_and(edge < HL, has_left), fore, 0.0)
                aft = jnp.where(jnp.logical_and(edge >= LANES - HL, has_right), aft, 0.0)
                blocks = [total[:, b : b + LANES] for b in range(0, C, LANES)]
                blocks[0] = blocks[0] + fore
                blocks[-1] = blocks[-1] + aft
                for b, block in enumerate(blocks):
                    out_ref[source * HS + h, rows, b * LANES : (b + 1) * LANES] = block
            return carry

        lax.fori_loop(0, HS, gather_step, 0)

    for copy in sends:
        copy.wait_send()
    for q in range(D):

        @pl.when(q != dep)
        def _():
            back_copy(q).wait_send()

        for side in (0, 1):
            spill_copy(side, q).wait_send()


def per_device(basis, factors, measured, shear, window):
    R, LD, H, C = basis.shape
    FB, W = factors.shape[0], measured.shape[2]
    T, D = lax.axis_size("tm"), lax.axis_size("depth")
    HS = H // D
    N = HS * C
    HL = 32
    while HL < SHEAR * (LD * D // 2):
        HL *= 2
    per = LANES // HL
    G = LD // per

    rows = jnp.transpose(basis, (2, 1, 0, 3)).reshape(D, HS, LD * R, C)

    def pack(columns):
        parts = columns.reshape(D, HS, G, per, R, HL)
        return jnp.transpose(parts, (0, 1, 2, 4, 3, 5)).reshape(D, HS, G * R, LANES)

    halo = jnp.stack([pack(rows[..., :HL]), pack(rows[..., C - HL :])])

    mine = lax.dynamic_slice_in_dim(measured, lax.axis_index("depth") * HS, HS, 1)
    mine = jnp.transpose(mine.reshape(FB, HS, T, C), (2, 0, 1, 3)).reshape(T, FB, N)
    low = window % 32
    facts = jnp.concatenate(
        [
            factors,
            jnp.stack([shear, window - low, low], 1).astype(jnp.bfloat16),
            jnp.zeros((FB, LANES - R - 3), jnp.bfloat16),
        ],
        1,
    )
    mine = jnp.concatenate([mine, jnp.broadcast_to(facts[None], (T, FB, LANES))], 2)

    bf, f32 = jnp.bfloat16, jnp.float32
    dma = pltpu.SemaphoreType.DMA
    out = pl.pallas_call(
        functools.partial(kernel, (T, D, LD, HS, C, R, HL, FB)),
        out_shape=jax.ShapeDtypeStruct((H, LD * R, C), f32),
        in_specs=[pl.BlockSpec(memory_space=pltpu.VMEM)] * 3,
        out_specs=pl.BlockSpec(memory_space=pltpu.VMEM),
        scratch_shapes=[
            pltpu.VMEM((D, HS, LD * R, C), bf),
            pltpu.VMEM((2, D, HS, G * R, LANES), bf),
            pltpu.VMEM((T, FB, N + LANES), bf),
            pltpu.VMEM((D, HS, LD * R, C), bf),
            pltpu.VMEM((2, D, HS, G * R, LANES), bf),
            pltpu.VMEM((D, HS, LD * R, C), bf),
            pltpu.VMEM((2, D, HS, G * R, LANES), bf),
            pltpu.VMEM((T * FB, 2 * LANES), bf),
            pltpu.VMEM((2 * LANES, N), f32),
            pltpu.VMEM((T * FB, N), f32),
            pltpu.VMEM((T * FB, N), bf),
            pltpu.VMEM((2 * LANES, N), f32),
            dma((D,)),
            dma((D,)),
            dma((2, D)),
            dma((2, D)),
            dma((T,)),
            dma((T,)),
            dma((D,)),
            dma((D,)),
            dma((2, D)),
            dma((2, D)),
        ],
        compiler_params=pltpu.CompilerParams(
            collective_id=0, has_side_effects=True, vmem_limit_bytes=40 * 1024 * 1024
        ),
    )(rows, halo, mine)
    return jnp.transpose(out.reshape(H, LD, R, C), (2, 1, 0, 3))


def solution(mesh):
    in_specs = (P(None, "depth", None, "tm"), P("tm", None), P("tm", None, None), P("tm"), P("tm"))
    out_specs = P(None, "depth", None, "tm")
    return jax.shard_map(
        per_device, mesh=mesh, in_specs=in_specs, out_specs=out_specs, check_vma=False
    )
```

time: 260 us -> 56.6 us (0.22)
  the two profiles are of different devices: /device:TPU:16 before, /device:TPU:25 now
where the time goes in v1:
time: 56.6 us; the launch traced here: 56.3 us
  Pallas kernels  41.9 us (74%)
  local copies, waits for them, and re-layouts  11.2 us (20%)
  other arithmetic  3.08 us (5%)
    pallas_call x1, Pallas kernels, per_device(): pl.pallas_call(functools.partial(kernel, (T, D, LD, HS, C, R, HL, FB)), o...  41.9 us
    another operation x3, other arithmetic, per_device(): jnp.stack([shear, window - low, low], 1).astype(jnp.bfloat16)  2.13 us
    unnamed x5, local copies, waits for them, and re-layouts  1.76 us
    another operation x2, local copies, waits for them, and re-layouts, per_device(): halo = jnp.stack([pack(rows[..., :HL]), pack(rows[..., C - HL:])])  1.59 us
    reshape x1, local copies, waits for them, and re-layouts, per_device(): return jnp.transpose(out.reshape(H, LD, R, C), (2, 1, 0, 3))  1.58 us
    reshape x1, local copies, waits for them, and re-layouts, per_device(): jnp.transpose(mine.reshape(FB, HS, T, C), (2, 0, 1, 3)).reshape(T, FB, N)  1.37 us
    reshape x2, local copies, waits for them, and re-layouts, pack(): parts = columns.reshape(D, HS, G, per, R, HL)  1.22 us
    transpose x1, local copies, waits for them, and re-layouts, per_device(): jnp.transpose(mine.reshape(FB, HS, T, C), (2, 0, 1, 3)).reshape(T, FB, N)  1.2 us

profile of v1, /device:TPU:25, one launch (start us, length us, event | category | flops | bytes accessed | tf_op | source)
XLA Modules:
  0.0 56.3 jit_solution(18090495487738203221)
XLA Ops:
  0.0 0.0 copy-start
  0.0 0.8 %convert_bitcast_fusion.2 = bf16[64,1]{0,1:T(2,128)(2,1)S(1)} fusion(s32[64]{0:T(128)} %param.8), kind=kLoop, calls=%fused_computation.11 | loop fusion | flops 64 | bytes 384 | tf_op jit(solution)/shard_map/stack | solution.py:349
  0.8 0.7 %convert_bitcast_fusion = (bf16[64,1]{0,1:T(2,128)(2,1)S(1)}, s32[64]{0:T(128)S(1)}) fusion(s32[64]{0:T(128)} %param.9), kind=kLoop, calls=%fused_computation.9 | loop fusion | flops 768 | bytes 640 | tf_op jit(solution)/shard_map/stack | solution.py:349
  1.5 0.7 %convert_bitcast_fusion.1 = bf16[64,1]{0,1:T(2,128)(2,1)S(1)} fusion(s32[64]{0:T(128)} %param.9, s32[64]{0:T(128)S(1)} %get-tuple-element.6), kind=kLoop, calls=%fused_computation.10 | loop fusion | flops 128 | bytes 640 | tf_op jit(solution)/shard_map/stack | solution.py:349
  2.1 0.1 copy.21
  2.3 0.1 copy.22
  2.4 0.1 copy.20
  2.5 0.8 %copy.19 = bf16[64,32]{1,0:T(8,128)(2,1)S(1)} copy(bf16[64,32]{0,1:T(8,128)(2,1)} %param.6) | data formatting | bytes 8192 | tf_op args[1]
  3.3 0.1 concatenate.7
  3.4 0.0 copy-done
  3.4 0.6 constant_dynamic-slice_fusion
  4.0 0.3 reshape.25
  4.3 1.2 %copy.18 = bf16[8,64,2,256]{3,2,1,0:T(2,128)(2,1)} copy(bf16[8,64,2,256]{3,0,2,1:T(8,128)(2,1)S(1)} %bitcast.29) | data formatting | bytes 1048576 | tf_op jit(solution)/shard_map/transpose | solution.py:344
  5.5 1.4 %reshape.23 = bf16[8,64,512]{2,1,0:T(8,128)(2,1)S(1)} reshape(bf16[8,64,2,256]{3,2,1,0:T(2,128)(2,1)} %copy.18) | data formatting | bytes 1048576 | tf_op jit(solution)/shard_map/reshape | solution.py:344
  6.9 0.0 copy-start.1
  6.9 0.1 pad_maximum_fusion.meas_ref
  7.0 1.0 %copy-done.1 = bf16[32,4,8,256]{3,2,1,0:T(8,128)(2,1)S(1)} copy-done((bf16[32,4,8,256]{3,2,1,0:T(8,128)(2,1)S(1)}, bf16[32,4,8,256]{3,2,1,0:T(8,128)(2,1)}, u32[]{:S(2)}) %copy-start.1) | copy-done | bytes 524312
  7.9 0.3 copy.14
  8.2 0.9 %fusion.1 = (bf16[4,2,128,32]{3,2,1,0:T(8,128)(2,1)S(1)}, bf16[4,2,128,32]{3,2,1,0:T(8,128)(2,1)}) fusion(bf16[4,2,128,256]{3,2,1,0:T(8,128)(2,1)S(1)} %bitcast.26), kind=kLoop, calls=%fused_computation.13 | loop fusion | bytes 262144 | tf_op jit(solution)/shard_map/slice | solution.py:341
  9.1 0.1 copy.31
  9.2 0.8 %stack_reshape.6 = bf16[1,4,2,32,128]{4,3,2,1,0:T(8,128)(2,1)} reshape(bf16[4,2,1,32,4,32]{5,4,3,1,0,2:T(4,128)(2,1)S(1)} %bitcast.30) | data formatting | bytes 131072 | tf_op jit(solution)/shard_map/stack;reshape | solution.py:341
  10.0 1.1 %copy.30 = bf16[4,2,1,4,32,32]{5,3,4,1,0,2:T(4,128)(2,1)S(1)} copy(bf16[4,2,1,4,32,32]{5,4,3,1,0,2:T(8,128)(2,1)} %bitcast.32) | data formatting | bytes 131072 | tf_op jit(solution)/shard_map/reshape | solution.py:338
  11.1 0.8 %stack_reshape.7 = bf16[1,4,2,32,128]{4,3,2,1,0:T(8,128)(2,1)} reshape(bf16[4,2,1,32,4,32]{5,4,3,1,0,2:T(4,128)(2,1)S(1)} %bitcast.31) | data formatting | bytes 131072 | tf_op jit(solution)/shard_map/stack;reshape | solution.py:341
  11.9 0.9 %pad_maximum_fusion.1.halo_ref = bf16[2,4,2,32,128]{4,3,2,1,0:T(8,128)(2,1)S(1)} fusion(bf16[1,4,2,32,128]{4,3,2,1,0:T(8,128)(2,1)} %stack_reshape.7, bf16[1,4,2,32,128]{4,3,2,1,0:T(8,128)(2,1)} %stack_reshape.6), kind=kLoop, calls=%fused_computation.4 | loop fusion | flops 65536 | bytes 262144 | tf_op jit(solution)/shard_map/stack | solution.py:341
  12.8 41.9 %shard_map.55 = f32[8,128,256]{2,1,0:T(8,128)S(1)} custom-call(bf16[4,2,128,256]{3,2,1,0:T(8,128)(2,1)S(1)} %bitcast.27, bf16[2,4,2,32,128]{4,3,2,1,0:T(8,128)(2,1)S(1)} %pad_maximum_fusion.1.halo_ref, bf16[8,64,640]{2,1,0:T(8,128)(2,1)S(1)} %pad_maximum_fusion.meas_ref), custom_call_target="tpu_custom_call" | custom-call | tf_op jit(solution)/shard_map/pallas_call | solution.py:358
  54.7 1.6 %copy.29 = f32[8,4,32,256]{3,0,1,2:T(8,128)} copy(f32[8,4,32,256]{3,2,1,0:T(8,128)S(1)} %bitcast.28) | data formatting | bytes 2097152 | tf_op jit(solution)/shard_map/reshape | solution.py:391
  (2 shorter events, 0.0 us)
Async XLA Ops:
  0.0 3.4 %copy-start = (bf16[64,8,2048]{2,1,0:T(8,128)(2,1)S(1)}, bf16[64,8,2048]{2,1,0:T(8,128)(2,1)}, u32[]{:S(2)}) copy-start(bf16[64,8,2048]{2,1,0:T(8,128)(2,1)} %param.7) | copy-start | bytes 6291460
  6.9 1.0 %copy-start.1 = (bf16[32,4,8,256]{3,2,1,0:T(8,128)(2,1)S(1)}, bf16[32,4,8,256]{3,2,1,0:T(8,128)(2,1)}, u32[]{:S(2)}) copy-start(bf16[32,4,8,256]{3,2,1,0:T(8,128)(2,1)} %param.5) | copy-start | bytes 1572868

commit v2 on v1

v2 whole, which is shorter than its diff:
```python
import functools
import math

import jax
import jax.numpy as jnp
from jax import lax
from jax.experimental import pallas as pl
from jax.experimental.pallas import tpu as pltpu
from jax.sharding import PartitionSpec as P

SHEAR = 3
WD = 1024
LANES = 128
STEPS = 2 * SHEAR + 1


def kernel(
    dims,
    main_ref,
    fact_ref,
    shear_ref,
    window_ref,
    meas_ref,
    out_ref,
    meas_all,
    snd_halo,
    snd_meas,
    in_main,
    in_halo,
    in_meas,
    back_main,
    back_spill,
    got_main,
    got_spill,
    coef,
    sheared,
    proj,
    grad,
    spread,
    load_sem,
    send_main,
    recv_main,
    send_halo,
    recv_halo,
    send_meas,
    recv_meas,
    send_out,
    recv_out,
    send_spill,
    recv_spill,
):
    T, D, LD, HS, C, R, HL, FB, H = dims
    N = HS * C
    WIDE = C + LANES
    per = LANES // HL
    G = LD // per
    half = LD * D // 2
    me = lax.axis_index("tm")
    dep = lax.axis_index("depth")
    left = lax.rem(me + T - 1, T)
    right = lax.rem(me + 1, T)
    outward = []
    for q in range((D + 1) // 2):
        outward += [q] if q == D - 1 - q else [q, D - 1 - q]

    def peer(base, k, n):
        return lax.rem(base + k, n)

    def at(tm, depth):
        return {"tm": tm, "depth": depth}

    def remote(src, dst, send, recv, where):
        return pltpu.make_async_remote_copy(
            src_ref=src,
            dst_ref=dst,
            send_sem=send,
            recv_sem=recv,
            device_id=where,
            device_id_type=pl.DeviceIdType.MESH,
        )

    load = pltpu.make_async_copy(meas_ref, meas_all, load_sem)
    load.start()

    barrier = pltpu.get_barrier_semaphore()
    greeted = 0
    for k in range(1, T):
        pl.semaphore_signal(
            barrier, inc=1, device_id=at(peer(me, k, T), dep), device_id_type=pl.DeviceIdType.MESH
        )
        greeted += 1
    for k in range(1, D):
        for tm in (me, left, right):
            pl.semaphore_signal(
                barrier, inc=1, device_id=at(tm, peer(dep, k, D)), device_id_type=pl.DeviceIdType.MESH
            )
            greeted += 1

    edge = lax.broadcasted_iota(jnp.int32, (R, LANES), 1)
    has_right = me < T - 1
    has_left = me > 0
    blank = jnp.zeros((R, LANES), jnp.float32)

    def pack(blocks_low, blocks_high):
        low = blank
        high = blank
        for p in range(per):
            fore = jnp.where(edge < HL, blocks_low[p], 0.0)
            aft = jnp.where(edge >= LANES - HL, blocks_high[p], 0.0)
            low = low + (pltpu.roll(fore, p * HL, 1) if p else fore)
            turn = (p * HL + HL) % LANES
            high = high + (pltpu.roll(aft, turn, 1) if turn else aft)
        return low.astype(jnp.bfloat16), high.astype(jnp.bfloat16)

    def pack_step(n, carry):
        q = n // HS
        h = n % HS
        for g in range(G):
            heads = []
            tails = []
            for p in range(per):
                rows = slice((g * per + p) * R, (g * per + p + 1) * R)
                heads.append(main_ref[q, h, rows, :LANES].astype(jnp.float32))
                tails.append(main_ref[q, h, rows, C - LANES :].astype(jnp.float32))
            low, high = pack(heads, tails)
            snd_halo[0, q, h, g * R : (g + 1) * R, :] = low
            snd_halo[1, q, h, g * R : (g + 1) * R, :] = high
        return carry

    lax.fori_loop(0, D * HS, pack_step, 0)
    in_main[dep] = main_ref[dep]
    pl.semaphore_wait(barrier, greeted)

    def main_copy(k, h):
        to = peer(dep, k, D)
        return remote(
            main_ref.at[to, h], in_main.at[dep, h], send_main.at[k, h], recv_main.at[dep, h], at(me, to)
        )

    def halo_copy(side, k, h):
        to = peer(dep, k, D)
        return remote(
            snd_halo.at[side, to, h],
            in_halo.at[side, dep, h],
            send_halo.at[side, k, h],
            recv_halo.at[side, dep, h],
            at((left, right)[side], to),
        )

    def meas_copy(k):
        to = peer(me, k, T)
        return remote(snd_meas.at[to], in_meas.at[me], send_meas.at[k], recv_meas.at[me], at(to, dep))

    def send_step(h, carry):
        for k in list(range(1, D)) + [0]:
            if k:
                main_copy(k, h).start()
            for side in (0, 1):
                halo_copy(side, k, h).start()
        return carry

    lax.fori_loop(0, HS, send_step, 0)

    row = lax.broadcasted_iota(jnp.int32, (FB, FB), 0)
    diagonal = row == lax.broadcasted_iota(jnp.int32, (FB, FB), 1)

    def upright(values):
        spread_out = jnp.broadcast_to(values.astype(jnp.float32), (FB, FB))
        return jnp.sum(jnp.where(diagonal, spread_out, 0.0), axis=1, keepdims=True)

    low_bits = window_ref[...] & 31
    lane = lax.broadcasted_iota(jnp.int32, (FB, LANES), 1)
    pick = lax.broadcasted_iota(jnp.int32, (R, LANES), 0) == edge
    pick = jnp.where(pick, 1.0, 0.0).astype(jnp.bfloat16)
    facts = lax.dot_general(
        fact_ref[...], pick, (((0,), (0,)), ((), ())), preferred_element_type=jnp.float32
    )
    facts = jnp.where(lane == R, upright(shear_ref[...]), facts)
    facts = jnp.where(lane == R + 1, upright(window_ref[...] - low_bits), facts)
    facts = jnp.where(lane == R + 2, upright(low_bits), facts)
    facts = facts.astype(jnp.bfloat16)

    wanted = lax.broadcasted_iota(jnp.int32, (HS * FB, FB * H), 0)
    wanted = lax.rem(wanted, FB) * H + dep * HS + lax.div(wanted, FB)
    select = wanted == lax.broadcasted_iota(jnp.int32, (HS * FB, FB * H), 1)
    select = jnp.where(select, 1.0, 0.0).astype(jnp.bfloat16)
    load.wait()
    for j in range(T):
        picked = jnp.dot(
            select, meas_all[:, j * C : (j + 1) * C], preferred_element_type=jnp.float32
        ).astype(jnp.bfloat16)
        for h in range(HS):
            snd_meas[j, :, h * C : (h + 1) * C] = picked[h * FB : (h + 1) * FB, :]
        snd_meas[j, :, N:] = facts

    for k in range(1, T):
        meas_copy(k).start()
    in_meas[me] = snd_meas[me]
    for k in range(1, T):
        source = peer(me, k, T)
        remote(
            snd_meas.at[source], in_meas.at[source], send_meas.at[k], recv_meas.at[source], at(source, dep)
        ).wait_recv()

    group = (lane // R).astype(jnp.float32)

    def coef_step(j, carry):
        info = in_meas[j, :, N:].astype(jnp.float32)
        first = jnp.where(lane < R, info, 0.0)
        tiled = first
        for q in range(1, LANES // R):
            tiled = tiled + pltpu.roll(first, q * R, 1)
        step = info[:, R : R + 1] + float(SHEAR)
        rows = pl.ds(pl.multiple_of(j * FB, FB), FB)
        for b in range(2):
            coef[rows, b * LANES : (b + 1) * LANES] = jnp.where(
                step == group + float(b * (LANES // R)), tiled, 0.0
            ).astype(jnp.bfloat16)
        return carry

    lax.fori_loop(0, T, coef_step, 0)

    norm_scale = 1.0 / math.sqrt(T * FB)
    column = lax.broadcasted_iota(jnp.int32, (FB, C), 1) + me * C
    column = column.astype(jnp.float32)

    def back_copy(q, h):
        return remote(
            back_main.at[q, h], got_main.at[dep, h], send_out.at[q, h], recv_out.at[dep, h], at(me, q)
        )

    def spill_copy(side, q, h):
        return remote(
            back_spill.at[side, q, h],
            got_spill.at[side, dep, h],
            send_spill.at[side, q, h],
            recv_spill.at[side, dep, h],
            at((right, left)[side], q),
        )

    def row_step(h, carry):
        columns = pl.ds(pl.multiple_of(h * C, LANES), C)
        sheared[...] = jnp.zeros_like(sheared)
        for q in outward[::-1]:

            @pl.when(q != dep)
            def _():
                remote(
                    main_ref.at[q, h], in_main.at[q, h], send_main.at[0, h], recv_main.at[q, h], at(me, q)
                ).wait_recv()

            for side in (0, 1):
                remote(
                    snd_halo.at[side, q, h],
                    in_halo.at[side, q, h],
                    send_halo.at[side, 0, h],
                    recv_halo.at[side, q, h],
                    at((right, left)[side], q),
                ).wait_recv()
            wides = []
            for l in range(LD):
                g, p = divmod(l, per)
                body = in_main[q, h, l * R : (l + 1) * R, :].astype(jnp.float32)
                after = in_halo[0, q, h, g * R : (g + 1) * R, :].astype(jnp.float32)
                before = in_halo[1, q, h, g * R : (g + 1) * R, :].astype(jnp.float32)
                after = pltpu.roll(after, (LANES - p * HL) % LANES, 1)
                before = pltpu.roll(before, (2 * LANES - HL - p * HL) % LANES, 1)
                rim = jnp.where(
                    jnp.logical_and(edge < HL, has_right),
                    after,
                    jnp.where(jnp.logical_and(edge >= LANES - HL, has_left), before, 0.0),
                )
                wides.append(jnp.concatenate([body, rim], axis=1))
            for s in range(STEPS):
                total = sheared[s * R : (s + 1) * R, :]
                for l in range(LD):
                    shift = (s - SHEAR) * (q * LD + l - half)
                    turned = pltpu.roll(wides[l], (-shift) % WIDE, 1) if shift else wides[l]
                    total = total + turned[:, :C]
                sheared[s * R : (s + 1) * R, :] = total

        table = sheared[...]
        high = table.astype(jnp.bfloat16)
        low = (table - high.astype(jnp.float32)).astype(jnp.bfloat16)
        proj[...] = jnp.dot(coef[...], high, preferred_element_type=jnp.float32) + jnp.dot(
            coef[...], low, preferred_element_type=jnp.float32
        )

        def ray_step(j, carry):
            rows = pl.ds(pl.multiple_of(j * FB, FB), FB)
            info = in_meas[j, :, N:].astype(jnp.float32)
            start = info[:, R + 1 : R + 2] + info[:, R + 2 : R + 3]
            transmit = jnp.exp(-proj[rows, :])
            inside = jnp.logical_and(column >= start, column < start + float(WD))
            residual = jnp.where(inside, transmit - in_meas[j, :, columns].astype(jnp.float32), 0.0)
            grad[rows, :] = (-transmit * residual * norm_scale).astype(jnp.bfloat16)
            return carry

        lax.fori_loop(0, T, ray_step, 0)
        spread[...] = lax.dot_general(
            coef[...], grad[...], (((0,), (0,)), ((), ())), preferred_element_type=jnp.float32
        )

        for q in outward:
            totals = [None] * LD
            for s in range(STEPS):
                piece = jnp.concatenate([spread[s * R : (s + 1) * R, :], blank], axis=1)
                for l in range(LD):
                    shift = (s - SHEAR) * (q * LD + l - half)
                    turned = pltpu.roll(piece, shift % WIDE, 1) if shift else piece
                    totals[l] = turned if s == 0 else totals[l] + turned
            for l in range(LD):
                back_main[q, h, l * R : (l + 1) * R, :] = totals[l][:, :C].astype(jnp.bfloat16)

            @pl.when(q == dep)
            def _():
                for l in range(LD):
                    out_ref[dep * HS + h, l * R : (l + 1) * R, :] = totals[l][:, :C]

            @pl.when(q != dep)
            def _():
                back_copy(q, h).start()

            for g in range(G):
                rims = [totals[g * per + p][:, C:] for p in range(per)]
                ahead, behind = pack(rims, rims)
                back_spill[0, q, h, g * R : (g + 1) * R, :] = ahead
                back_spill[1, q, h, g * R : (g + 1) * R, :] = behind
            for side in (0, 1):
                spill_copy(side, q, h).start()
        return carry

    lax.fori_loop(0, HS, row_step, 0)

    def gather_step(h, carry):
        for k in range(D):
            source = peer(dep, k, D)
            if k:
                remote(
                    back_main.at[source, h],
                    got_main.at[source, h],
                    send_out.at[0, h],
                    recv_out.at[source, h],
                    at(me, source),
                ).wait_recv()
            for side in (0, 1):
                remote(
                    back_spill.at[side, source, h],
                    got_spill.at[side, source, h],
                    send_spill.at[side, 0, h],
                    recv_spill.at[side, source, h],
                    at((left, right)[side], source),
                ).wait_recv()
            for l in range(LD):
                g, p = divmod(l, per)
                rows = slice(l * R, (l + 1) * R)
                if k:
                    total = got_main[source, h, rows, :].astype(jnp.float32)
                else:
                    total = out_ref[source * HS + h, rows, :]
                fore = got_spill[0, source, h, g * R : (g + 1) * R, :].astype(jnp.float32)
                aft = got_spill[1, source, h, g * R : (g + 1) * R, :].astype(jnp.float32)
                fore = pltpu.roll(fore, (LANES - p * HL) % LANES, 1)
                aft = pltpu.roll(aft, (2 * LANES - HL - p * HL) % LANES, 1)
                fore = jnp.where(jnp.logical_and(edge < HL, has_left), fore, 0.0)
                aft = jnp.where(jnp.logical_and(edge >= LANES - HL, has_right), aft, 0.0)
                blocks = [total[:, b : b + LANES] for b in range(0, C, LANES)]
                blocks[0] = blocks[0] + fore
                blocks[-1] = blocks[-1] + aft
                for b, block in enumerate(blocks):
                    out_ref[source * HS + h, rows, b * LANES : (b + 1) * LANES] = block
        return carry

    lax.fori_loop(0, HS, gather_step, 0)

    for k in range(1, T):
        meas_copy(k).wait_send()

    def drain_step(h, carry):
        for k in range(D):
            if k:
                main_copy(k, h).wait_send()
            for side in (0, 1):
                halo_copy(side, k, h).wait_send()
        for q in range(D):

            @pl.when(q != dep)
            def _():
                back_copy(q, h).wait_send()

            for side in (0, 1):
                spill_copy(side, q, h).wait_send()
        return carry

    lax.fori_loop(0, HS, drain_step, 0)


def per_device(basis, factors, measured, shear, window):
    R, LD, H, C = basis.shape
    FB, W = factors.shape[0], measured.shape[2]
    T, D = lax.axis_size("tm"), lax.axis_size("depth")
    HS = H // D
    N = HS * C
    HL = 32
    while HL < SHEAR * (LD * D // 2):
        HL *= 2
    G = LD // (LANES // HL)

    rows = jnp.transpose(basis, (2, 1, 0, 3)).reshape(D, HS, LD * R, C)

    bf, f32 = jnp.bfloat16, jnp.float32
    dma = pltpu.SemaphoreType.DMA
    whole = pl.BlockSpec(memory_space=pltpu.VMEM)
    out = pl.pallas_call(
        functools.partial(kernel, (T, D, LD, HS, C, R, HL, FB, H)),
        out_shape=jax.ShapeDtypeStruct((H, LD * R, C), f32),
        in_specs=[whole, whole, whole, whole, pl.BlockSpec(memory_space=pl.ANY)],
        out_specs=whole,
        scratch_shapes=[
            pltpu.VMEM((FB * H, W), bf),
            pltpu.VMEM((2, D, HS, G * R, LANES), bf),
            pltpu.VMEM((T, FB, N + LANES), bf),
            pltpu.VMEM((D, HS, LD * R, C), bf),
            pltpu.VMEM((2, D, HS, G * R, LANES), bf),
            pltpu.VMEM((T, FB, N + LANES), bf),
            pltpu.VMEM((D, HS, LD * R, C), bf),
            pltpu.VMEM((2, D, HS, G * R, LANES), bf),
            pltpu.VMEM((D, HS, LD * R, C), bf),
            pltpu.VMEM((2, D, HS, G * R, LANES), bf),
            pltpu.VMEM((T * FB, 2 * LANES), bf),
            pltpu.VMEM((2 * LANES, C), f32),
            pltpu.VMEM((T * FB, C), f32),
            pltpu.VMEM((T * FB, C), bf),
            pltpu.VMEM((2 * LANES, C), f32),
            dma,
            dma((D, HS)),
            dma((D, HS)),
            dma((2, D, HS)),
            dma((2, D, HS)),
            dma((T,)),
            dma((T,)),
            dma((D, HS)),
            dma((D, HS)),
            dma((2, D, HS)),
            dma((2, D, HS)),
        ],
        compiler_params=pltpu.CompilerParams(
            collective_id=0, has_side_effects=True, vmem_limit_bytes=60 * 1024 * 1024
        ),
    )(rows, factors.T, shear.reshape(1, FB), window.reshape(1, FB), measured.reshape(FB * H, W))
    return jnp.transpose(out.reshape(H, LD, R, C), (2, 1, 0, 3))


def solution(mesh):
    in_specs = (P(None, "depth", None, "tm"), P("tm", None), P("tm", None, None), P("tm"), P("tm"))
    out_specs = P(None, "depth", None, "tm")
    return jax.shard_map(
        per_device, mesh=mesh, in_specs=in_specs, out_specs=out_specs, check_vma=False
    )
```

time: 56.6 us -> 43.7 us (0.77)
  the two profiles are of different devices: /device:TPU:25 before, /device:TPU:16 now
where the time goes in v2:
time: 43.7 us; the launch traced here: 43.5 us
  Pallas kernels  38.6 us (88%)
  local copies, waits for them, and re-layouts  4.93 us (11%)
    pallas_call x1, Pallas kernels, per_device(): pl.pallas_call(functools.partial(kernel, (T, D, LD, HS, C, R, HL, FB, H))...  38.6 us
    reshape x1, local copies, waits for them, and re-layouts, per_device(): return jnp.transpose(out.reshape(H, LD, R, C), (2, 1, 0, 3))  2.81 us
    transpose x1, local copies, waits for them, and re-layouts, per_device(): rows = jnp.transpose(basis, (2, 1, 0, 3)).reshape(D, HS, LD * R, C)  2.13 us

profile of v2, /device:TPU:16, one launch (start us, length us, event | category | flops | bytes accessed | tf_op | source)
XLA Modules:
  0.0 43.5 jit_solution(13772921718222774947)
XLA Ops:
  0.0 2.1 %copy.6 = bf16[8,4,32,256]{3,2,1,0:T(8,128)(2,1)} copy(bf16[8,4,32,256]{3,0,1,2:T(8,128)(2,1)} %bitcast.13) | data formatting | bytes 1048576 | tf_op jit(solution)/shard_map/transpose | solution.py:409
  2.1 38.6 %shard_map.55 = f32[8,128,256]{2,1,0:T(8,128)} custom-call(bf16[4,2,128,256]{3,2,1,0:T(8,128)(2,1)} %bitcast.12, bf16[32,64]{1,0:T(8,128)(2,1)} %bitcast.14, s32[1,64]{1,0:T(1,128)} %bitcast.15, s32[1,64]{1,0:T(1,128)} %bitcast.16, bf16[512,2048]{1,0:T(8,128)(2,1)} %bitcast.11), custom_call_target="tpu_custom_call" | custom-call | tf_op jit(solution)/shard_map/pallas_call | solution.py:414
  40.7 2.8 %copy.9 = f32[8,4,32,256]{3,0,1,2:T(8,128)} copy(f32[8,4,32,256]{3,2,1,0:T(8,128)} %bitcast.10) | data formatting | bytes 2097152 | tf_op jit(solution)/shard_map/reshape | solution.py:451

commit v3 on v2

--- a/solution.py
+++ b/solution.py
@@ -16,12 +16,14 @@
 
 def kernel(
     dims,
-    main_ref,
+    basis_ref,
     fact_ref,
     shear_ref,
     window_ref,
     meas_ref,
     out_ref,
+    flat,
+    main_ref,
     meas_all,
     snd_halo,
     snd_meas,
@@ -96,6 +98,19 @@
             )
             greeted += 1
 
+    count = R * LD * H
+    for c in range(C // LANES):
+        flat[c * count : (c + 1) * count, :] = basis_ref[:, c * LANES : (c + 1) * LANES].astype(
+            jnp.float32
+        )
+    for c in range(C // LANES):
+        for h in range(H):
+            for l in range(LD):
+                rows = flat[pl.ds(c * count + l * H + h, R, stride=LD * H), :]
+                main_ref[
+                    h // HS, h % HS, l * R : (l + 1) * R, c * LANES : (c + 1) * LANES
+                ] = rows.astype(jnp.bfloat16)
+
     edge = lax.broadcasted_iota(jnp.int32, (R, LANES), 1)
     has_right = me < T - 1
     has_left = me > 0
@@ -127,8 +142,6 @@
             snd_halo[1, q, h, g * R : (g + 1) * R, :] = high
         return carry
 
-    lax.fori_loop(0, D * HS, pack_step, 0)
-    in_main[dep] = main_ref[dep]
     pl.semaphore_wait(barrier, greeted)
 
     def main_copy(k, h):
@@ -151,15 +164,16 @@
         to = peer(me, k, T)
         return remote(snd_meas.at[to], in_meas.at[me], send_meas.at[k], recv_meas.at[me], at(to, dep))
 
-    def send_step(h, carry):
+    for k in range(1, D):
+        main_copy(k, 0).start()
+    lax.fori_loop(0, D * HS, pack_step, 0)
+    for h in range(HS):
         for k in list(range(1, D)) + [0]:
-            if k:
+            if k and h:
                 main_copy(k, h).start()
             for side in (0, 1):
                 halo_copy(side, k, h).start()
-        return carry
-
-    lax.fori_loop(0, HS, send_step, 0)
+    in_main[dep] = main_ref[dep]
 
     row = lax.broadcasted_iota(jnp.int32, (FB, FB), 0)
     diagonal = row == lax.broadcasted_iota(jnp.int32, (FB, FB), 1)
@@ -406,8 +420,6 @@
         HL *= 2
     G = LD // (LANES // HL)
 
-    rows = jnp.transpose(basis, (2, 1, 0, 3)).reshape(D, HS, LD * R, C)
-
     bf, f32 = jnp.bfloat16, jnp.float32
     dma = pltpu.SemaphoreType.DMA
     whole = pl.BlockSpec(memory_space=pltpu.VMEM)
@@ -417,6 +429,8 @@
         in_specs=[whole, whole, whole, whole, pl.BlockSpec(memory_space=pl.ANY)],
         out_specs=whole,
         scratch_shapes=[
+            pltpu.VMEM((C // LANES * R * LD * H, LANES), f32),
+            pltpu.VMEM((D, HS, LD * R, C), bf),
             pltpu.VMEM((FB * H, W), bf),
             pltpu.VMEM((2, D, HS, G * R, LANES), bf),
             pltpu.VMEM((T, FB, N + LANES), bf),
@@ -447,7 +461,7 @@
         compiler_params=pltpu.CompilerParams(
             collective_id=0, has_side_effects=True, vmem_limit_bytes=60 * 1024 * 1024
         ),
-    )(rows, factors.T, shear.reshape(1, FB), window.reshape(1, FB), measured.reshape(FB * H, W))
+    )(basis.reshape(R * LD * H, C), factors.T, shear.reshape(1, FB), window.reshape(1, FB), measured.reshape(FB * H, W))
     return jnp.transpose(out.reshape(H, LD, R, C), (2, 1, 0, 3))
 
 

time: 43.7 us -> 42.8 us (0.979)
  local copies, waits for them, and re-layouts: 4.93 us -> 2.81 us
  Pallas kernels: 38.6 us -> 39.8 us
    transpose x1 -> x0, local copies, waits for them, and re-layouts: 2.13 us -> none  [per_device(): rows = jnp.transpose(basis, (2, 1, 0, 3)).reshape(D, HS, LD * R, C)]
    pallas_call x1, Pallas kernels: 38.6 us -> 39.8 us  [per_device(): pl.pallas_call(functools.partial(kernel, (T, D, LD, HS, C, R, HL, FB, H))...]
where the time goes in v3:
time: 42.8 us; the launch traced here: 42.6 us
  Pallas kernels  39.8 us (93%)
  local copies, waits for them, and re-layouts  2.81 us (7%)
    pallas_call x1, Pallas kernels, per_device(): pl.pallas_call(functools.partial(kernel, (T, D, LD, HS, C, R, HL, FB, H))...  39.8 us
    reshape x1, local copies, waits for them, and re-layouts, per_device(): return jnp.transpose(out.reshape(H, LD, R, C), (2, 1, 0, 3))  2.81 us

profile of v3, /device:TPU:16, one launch (start us, length us, event | category | flops | bytes accessed | tf_op | source)
XLA Modules:
  0.0 42.6 jit_solution(15096577517445561240)
XLA Ops:
  0.0 39.8 %shard_map.55 = f32[8,128,256]{2,1,0:T(8,128)} custom-call(bf16[1024,256]{1,0:T(8,128)(2,1)} %bitcast.11, bf16[32,64]{1,0:T(8,128)(2,1)} %bitcast.12, s32[1,64]{1,0:T(1,128)} %bitcast.13, s32[1,64]{1,0:T(1,128)} %bitcast.14, bf16[512,2048]{1,0:T(8,128)(2,1)} %bitcast.10), custom_call_target="tpu_custom_call" | custom-call | tf_op jit(solution)/shard_map/pallas_call | solution.py:426
  39.8 2.8 %copy.8 = f32[8,4,32,256]{3,0,1,2:T(8,128)} copy(f32[8,4,32,256]{3,2,1,0:T(8,128)} %bitcast.9) | data formatting | bytes 2097152 | tf_op jit(solution)/shard_map/reshape | solution.py:465

commit v4 on v3

--- a/solution.py
+++ b/solution.py
@@ -22,6 +22,8 @@
     window_ref,
     meas_ref,
     out_ref,
+    own,
+    placed,
     flat,
     main_ref,
     meas_all,
@@ -329,7 +331,7 @@
             @pl.when(q == dep)
             def _():
                 for l in range(LD):
-                    out_ref[dep * HS + h, l * R : (l + 1) * R, :] = totals[l][:, :C]
+                    own[h, l * R : (l + 1) * R, :] = totals[l][:, :C]
 
             @pl.when(q != dep)
             def _():
@@ -371,7 +373,7 @@
                 if k:
                     total = got_main[source, h, rows, :].astype(jnp.float32)
                 else:
-                    total = out_ref[source * HS + h, rows, :]
+                    total = own[h, rows, :]
                 fore = got_spill[0, source, h, g * R : (g + 1) * R, :].astype(jnp.float32)
                 aft = got_spill[1, source, h, g * R : (g + 1) * R, :].astype(jnp.float32)
                 fore = pltpu.roll(fore, (LANES - p * HL) % LANES, 1)
@@ -382,10 +384,13 @@
                 blocks[0] = blocks[0] + fore
                 blocks[-1] = blocks[-1] + aft
                 for b, block in enumerate(blocks):
-                    out_ref[source * HS + h, rows, b * LANES : (b + 1) * LANES] = block
+                    first = b * count + l * H + source * HS + h
+                    placed[pl.ds(first, R, stride=LD * H), :] = block
         return carry
 
     lax.fori_loop(0, HS, gather_step, 0)
+    for c in range(C // LANES):
+        out_ref[:, c * LANES : (c + 1) * LANES] = placed[c * count : (c + 1) * count, :]
 
     for k in range(1, T):
         meas_copy(k).wait_send()
@@ -425,10 +430,12 @@
     whole = pl.BlockSpec(memory_space=pltpu.VMEM)
     out = pl.pallas_call(
         functools.partial(kernel, (T, D, LD, HS, C, R, HL, FB, H)),
-        out_shape=jax.ShapeDtypeStruct((H, LD * R, C), f32),
+        out_shape=jax.ShapeDtypeStruct((R * LD * H, C), f32),
         in_specs=[whole, whole, whole, whole, pl.BlockSpec(memory_space=pl.ANY)],
         out_specs=whole,
         scratch_shapes=[
+            pltpu.VMEM((HS, LD * R, C), f32),
+            pltpu.VMEM((C // LANES * R * LD * H, LANES), f32),
             pltpu.VMEM((C // LANES * R * LD * H, LANES), f32),
             pltpu.VMEM((D, HS, LD * R, C), bf),
             pltpu.VMEM((FB * H, W), bf),
@@ -462,7 +469,7 @@
             collective_id=0, has_side_effects=True, vmem_limit_bytes=60 * 1024 * 1024
         ),
     )(basis.reshape(R * LD * H, C), factors.T, shear.reshape(1, FB), window.reshape(1, FB), measured.reshape(FB * H, W))
-    return jnp.transpose(out.reshape(H, LD, R, C), (2, 1, 0, 3))
+    return out.reshape(R, LD, H, C)
 
 
 def solution(mesh):

time: 42.8 us -> 42.5 us (level)
  local copies, waits for them, and re-layouts: 2.81 us -> 2.31 us
    reshape x1 -> x0, local copies, waits for them, and re-layouts: 2.81 us -> none  [per_device(): return jnp.transpose(out.reshape(H, LD, R, C), (2, 1, 0, 3))]
    unnamed x0 -> x1, local copies, waits for them, and re-layouts: none -> 2.31 us
where the time goes in v4:
time: 42.5 us; the launch traced here: 42.3 us
  Pallas kernels  40 us (94%)
  local copies, waits for them, and re-layouts  2.31 us (5%)
    pallas_call x1, Pallas kernels, per_device(): pl.pallas_call(functools.partial(kernel, (T, D, LD, HS, C, R, HL, FB, H))...  40 us
    unnamed x1, local copies, waits for them, and re-layouts  2.31 us

profile of v4, /device:TPU:16, one launch (start us, length us, event | category | flops | bytes accessed | tf_op | source)
XLA Modules:
  0.0 42.3 jit_solution(15495885606580848555)
XLA Ops:
  0.0 40.0 %shard_map.55 = f32[1024,256]{1,0:T(8,128)} custom-call(bf16[1024,256]{1,0:T(8,128)(2,1)} %bitcast.8, bf16[32,64]{1,0:T(8,128)(2,1)} %bitcast.9, s32[1,64]{1,0:T(1,128)} %bitcast.10, s32[1,64]{1,0:T(1,128)} %bitcast.11, bf16[512,2048]{1,0:T(8,128)(2,1)} %bitcast.7), custom_call_target="tpu_custom_call" | custom-call | tf_op jit(solution)/shard_map/pallas_call | solution.py:431
  40.0 2.3 %copy.7 = f32[32,4,8,256]{3,2,1,0:T(8,128)} copy(f32[32,4,8,256]{3,2,1,0:T(8,128)} %bitcast.6) | data formatting | bytes 2097152
